TPU v7x, 32 devices: a whole 2x2x4 slice. The times are simulated.
32 devices in a mesh: dp: 8 (over z, core), fsdp: 4 (over y, x).
Axes of the slice: x: 2, y: 2, z: 4, core: 2. Of those that a mesh axis runs over, the one named last changes fastest.
Arguments:
- tokens: bfloat16 [512, 196, 432], P(('dp', 'fsdp')), may hold values from -6 to 6
- keep_mask: int32 [512, 196], P(('dp', 'fsdp')), may hold values from 0 to 1, as said below
- cotangent: bfloat16 [512, 196, 432], P(('dp', 'fsdp')), may hold values from -6 to 6
- qk_weight: float32 [432, 864], P('dp', 'fsdp'), may hold values from -0.3125 to 0.3125
- qk_first: float32 [432, 864], P('dp', 'fsdp'), may hold values from -0.00390625 to 0.00390625
- qk_second: float32 [432, 864], P('dp', 'fsdp'), may hold values from 4.4653063e-07 to 1.7861225e-06
- value_weight: float32 [432, 432], P('fsdp', 'dp'), may hold values from -0.3125 to 0.3125
- value_first: float32 [432, 432], P('fsdp', 'dp'), may hold values from -0.00390625 to 0.00390625
- value_second: float32 [432, 432], P('fsdp', 'dp'), may hold values from 4.4653063e-07 to 1.7861225e-06
- out_weight: float32 [432, 432], P('fsdp', 'dp'), may hold values from -0.625 to 0.625
- out_first: float32 [432, 432], P('fsdp', 'dp'), may hold values from -0.00390625 to 0.00390625
- out_second: float32 [432, 432], P('fsdp', 'dp'), may hold values from 4.4653063e-07 to 1.7861225e-06
- up_weight: float32 [432, 1728], P('fsdp', 'dp'), may hold values from -0.3125 to 0.3125
- up_first: float32 [432, 1728], P('fsdp', 'dp'), may hold values from -0.00390625 to 0.00390625
- up_second: float32 [432, 1728], P('fsdp', 'dp'), may hold values from 4.4653063e-07 to 1.7861225e-06
- down_weight: float32 [1728, 432], P('dp', 'fsdp'), may hold values from -0.15625 to 0.15625
- down_first: float32 [1728, 432], P('dp', 'fsdp'), may hold values from -0.00390625 to 0.00390625
- down_second: float32 [1728, 432], P('dp', 'fsdp'), may hold values from 4.4653063e-07 to 1.7861225e-06
- vectors: float32 [6, 432], P(None, 'fsdp'), may hold values from -1.2 to 2.45
- vectors_first: float32 [6, 432], P(None, 'fsdp'), may hold values from -0.01171875 to 0.01171875
- vectors_second: float32 [6, 432], P(None, 'fsdp'), may hold values from 4.0187756e-06 to 1.6075102e-05
- up_bias: float32 [1728], P('fsdp'), may hold values from -1.5 to 1.5
- up_bias_first: float32 [1728], P('fsdp'), may hold values from -0.00390625 to 0.00390625
- up_bias_second: float32 [1728], P('fsdp'), may hold values from 4.4653063e-07 to 1.7861225e-06
- locality: float32 [4, 9], replicated, may hold values from -3 to 3
- locality_first: float32 [4, 9], replicated, may hold values from -0.125 to 0.125
- locality_second: float32 [4, 9], replicated, may hold values from 0.00040187757 to 0.0016075103
Outputs:
- result: bfloat16 [512, 196, 432], P(('dp', 'fsdp'))
- token_grad: bfloat16 [512, 196, 432], P(('dp', 'fsdp'))
- grad_norm: float32 [], replicated
- qk_new: float32 [432, 864], P('dp', 'fsdp')
- qk_copy: bfloat16 [432, 864], P('dp', 'fsdp')
- qk_moment: float32 [432, 864], P('dp', 'fsdp')
- qk_square: float32 [432, 864], P('dp', 'fsdp')
- value_new: float32 [432, 432], P('fsdp', 'dp')
- value_copy: bfloat16 [432, 432], P('fsdp', 'dp')
- value_moment: float32 [432, 432], P('fsdp', 'dp')
- value_square: float32 [432, 432], P('fsdp', 'dp')
- out_new: float32 [432, 432], P('fsdp', 'dp')
- out_copy: bfloat16 [432, 432], P('fsdp', 'dp')
- out_moment: float32 [432, 432], P('fsdp', 'dp')
- out_square: float32 [432, 432], P('fsdp', 'dp')
- up_new: float32 [432, 1728], P('fsdp', 'dp')
- up_copy: bfloat16 [432, 1728], P('fsdp', 'dp')
- up_moment: float32 [432, 1728], P('fsdp', 'dp')
- up_square: float32 [432, 1728], P('fsdp', 'dp')
- down_new: float32 [1728, 432], P('dp', 'fsdp')
- down_copy: bfloat16 [1728, 432], P('dp', 'fsdp')
- down_moment: float32 [1728, 432], P('dp', 'fsdp')
- down_square: float32 [1728, 432], P('dp', 'fsdp')
- vectors_new: float32 [6, 432], P(None, 'fsdp')
- vectors_moment: float32 [6, 432], P(None, 'fsdp')
- vectors_square: float32 [6, 432], P(None, 'fsdp')
- up_bias_new: float32 [1728], P('fsdp')
- up_bias_moment: float32 [1728], P('fsdp')
- up_bias_square: float32 [1728], P('fsdp')
- locality_new: float32 [4, 9], replicated
- locality_moment: float32 [4, 9], replicated
- locality_square: float32 [4, 9], replicated
Inputs may be any that keep to these rules, and one draw needn't show every extreme that they name: `keep_mask`: every image keeps at least one of its 196 slots.
All inputs are finite; a program needn't handle non-finite values.
Results may differ from a plain program's by a relative error of at most 0.02.
Values may be sent and summed in bfloat16 or wider, within the bound.
A program may use at most 320 MiB of HBM per device.

v0:
```python
from functools import partial

import jax
import jax.numpy as jnp
from jax import lax
from jax.experimental import pallas as pl
from jax.experimental.pallas import tpu as pltpu
from jax.sharding import PartitionSpec as P

GRID = 14
STEP = 5
PITCH = 256

norm_eps = 1e-06
learn_rate = 0.03
small_rate = 0.3
beta_one = 0.5
beta_two = 0.5
adam_eps = 1e-08
weight_decay = 0.05
clip_limit = 1.0

LOG2E = 1.4426950408889634
PHI_ZERO = 0.3989422804014327

f32 = jnp.float32
bf16 = jnp.bfloat16


def mm(a, b):
    return lax.dot_general(a, b, (((1,), (0,)), ((), ())), preferred_element_type=f32)


def mm_nt(a, b):
    return lax.dot_general(a, b, (((1,), (1,)), ((), ())), preferred_element_type=f32)


def gelu_parts(u):
    v = u * 0.5**0.5
    cdf = 0.5 * lax.erf(v) + 0.5
    bell = jnp.exp2(v * v * -LOG2E)
    return u * cdf, cdf + (v * (PHI_ZERO * 2**0.5)) * bell


MESH = pl.DeviceIdType.MESH


def up16(v):
    return -(-v // 16) * 16


class Place:
    def __init__(self, dp, fsdp):
        self.cores = 2 if dp % 2 == 0 else 1
        self.zs = dp // self.cores
        self.ys = max(v for v in range(1, fsdp + 1) if fsdp % v == 0 and v * v <= fsdp)
        self.xs = fsdp // self.ys
        self.fs = fsdp
        at_dp, at_f = lax.axis_index("dp"), lax.axis_index("fsdp")
        self.z, self.c = at_dp // self.cores, at_dp % self.cores
        self.y, self.x = at_f // self.xs, at_f % self.xs

    def to(self, dz=0, dc=0, dy=0, dx=0):
        z = lax.rem(self.z + dz, self.zs)
        c = lax.rem(self.c + dc, self.cores)
        y = lax.rem(self.y + dy, self.ys)
        x = lax.rem(self.x + dx, self.xs)
        return (z * self.cores + c, y * self.xs + x)


def greet(peers):
    barrier = pltpu.get_barrier_semaphore()
    for peer in peers:
        pl.semaphore_signal(barrier, inc=1, device_id=peer, device_id_type=MESH)
    pl.semaphore_wait(barrier, len(peers))


def row_plan(fu, u):
    o_at = 2 * up16(fu)
    split = up16(o_at + u)
    return o_at, split, split + up16(3 * u)


class Gatherer:
    def __init__(self, here, rows, block, slots, send, recv):
        self.here, self.block, self.slots, self.send, self.recv = here, block, slots, send, recv
        half = rows // 32 * 16
        self.segs = (pl.ds(0, half), pl.ds(half, rows - half))
        self.keys = gatherer_keys(here.zs, here.ys, here.xs, here.cores)
        self.order = [0] + z_order(here.zs)[:-1]

    def slot(self, owner, seg):
        return self.slots.at[owner[0], owner[1], self.segs[seg]]

    def copy(self, key):
        here, kind, k, a, b, seg, to = self.here, *key
        owner = here.to(dz=k, dy=a, dx=b)
        own = (k, a, b) == (0, 0, 0)
        target = {"z": here.to(dz=to), "y": here.to(dy=to), "x": here.to(dx=to), "c": here.to(dc=to)}[kind]
        return pltpu.make_async_remote_copy(
            src_ref=self.block.at[self.segs[seg]] if own else self.slot(owner, seg),
            dst_ref=self.slot(owner, seg),
            send_sem=self.send.at[self.keys.index(key)],
            recv_sem=self.recv.at[owner[0] * here.fs + owner[1], seg],
            device_id=target,
            device_id_type=MESH,
        )

    def push(self, kind, k, a, b, seg):
        for key in self.keys:
            if key[:5] == (kind, k, a, b, seg):
                self.copy(key).start()

    def arrive(self, k, a, b, seg, dc=0):
        owner = self.here.to(dz=k, dy=a, dx=b, dc=dc)
        slot = self.slot(owner, seg)
        pltpu.make_async_remote_copy(
            src_ref=slot,
            dst_ref=slot,
            send_sem=self.send.at[0],
            recv_sem=self.recv.at[owner[0] * self.here.fs + owner[1], seg],
            device_id=self.here.to(),
            device_id_type=MESH,
        ).wait_recv()

    def spread(self, k):
        for kind in "yxc":
            for seg in (0, 1):
                self.push(kind, k, 0, 0, seg)

    def relay(self, k):
        here = self.here
        for a in range(1, here.ys):
            self.arrive(k, a, 0, 0)
            self.push("x", k, a, 0, 0)
        for b in range(1, here.xs):
            self.arrive(k, 0, b, 1)
            self.push("y", k, 0, b, 1)
        for a in range(1, here.ys):
            self.arrive(k, a, 0, 1)
            for seg in (0, 1):
                self.push("c", k, a, 0, seg)
        for b in range(1, here.xs):
            self.arrive(k, 0, b, 0)
            for seg in (0, 1):
                self.push("c", k, 0, b, seg)

    def corner(self, k):
        for a in range(1, self.here.ys):
            for b in range(1, self.here.xs):
                for seg in (0, 1):
                    self.arrive(k, a, b, seg)
                    self.push("c", k, a, b, seg)

    def twin(self, k):
        here = self.here
        for c in range(1, here.cores):
            for a in range(here.ys):
                for b in range(here.xs):
                    for seg in (0, 1):
                        self.arrive(k, a, b, seg, c)

    def events(self):
        return self.here.zs + 3

    def event(self, t):
        zs = self.here.zs
        if t == 0:
            for seg in (0, 1):
                self.push("z", 0, 0, 0, seg)
            self.spread(0)
        elif t < zs:
            for seg in (0, 1):
                self.arrive(self.order[t], 0, 0, seg)
            self.spread(self.order[t])
            self.relay(self.order[t - 1])
        elif t == zs:
            self.relay(self.order[zs - 1])
            for k in self.order[: zs // 2]:
                self.corner(k)
        elif t == zs + 1:
            for k in self.order[zs // 2 :]:
                self.corner(k)
        else:
            for k in self.order:
                self.twin(k)

    def finish(self):
        for key in self.keys:
            self.copy(key).wait_send()


def gatherer_keys(zs, ys, xs, cores):
    keys = [("z", 0, 0, 0, seg, k) for seg in (0, 1) for k in range(1, zs)]
    for k in range(zs):
        for seg in (0, 1):
            keys += [("y", k, 0, 0, seg, a) for a in range(1, ys)]
            keys += [("x", k, 0, 0, seg, b) for b in range(1, xs)]
        keys += [("x", k, a, 0, 0, b) for a in range(1, ys) for b in range(1, xs)]
        keys += [("y", k, 0, b, 1, a) for a in range(1, ys) for b in range(1, xs)]
        keys += [("c", k, a, b, seg, c) for a in range(ys) for b in range(xs) for seg in (0, 1) for c in range(1, cores)]
    return keys


def gather_kernel(dp, fsdp, rows, qk_ref, vt_ref, ot_ref, vec_ref, upb_ref, tok_ref, cot_ref, all_ref, small_ref, tok_out, cot_out, wide, block, part, slab, rows_s, turned_s, in_qk, in_vt, in_ot, in_vec, in_upb, in_sem, send, recv, small_send, small_recv, local, turn_sem):
    here = Place(dp, fsdp)
    zs, ys, xs, cores = here.zs, here.ys, here.xs, here.cores
    u, w = vt_ref.shape
    me = here.to()
    peers = [here.to(dz=k) for k in range(1, zs)] + [here.to(dc=k) for k in range(1, cores)]
    peers += [here.to(dy=a, dx=b) for a in range(ys) for b in range(xs) if a or b]

    loads = []
    for ref, into in ((qk_ref, in_qk), (vt_ref, in_vt), (ot_ref, in_ot), (vec_ref, in_vec), (upb_ref, in_upb)):
        loads.append(pltpu.make_async_copy(ref, into, in_sem.at[len(loads)]))
        loads[-1].start()
    slots, images, d = tok_ref.shape
    spans = [(lo, min(lo + 128, d)) for lo in range(0, d, 128)]
    arrivals = [pltpu.make_async_copy(ref, slab.at[n], turn_sem.at[n]) for n, ref in enumerate((tok_ref, cot_ref))]
    for copy in arrivals:
        copy.start()

    def widen_all(n):
        arrivals[n].wait()

        def widen(k, _):
            for c, (lo, hi) in enumerate(spans):
                rows_s[c, pl.ds(pl.multiple_of(k * images, 8), images), 0 : hi - lo] = slab[n, k, :, lo:hi].astype(f32)
            return 0

        lax.fori_loop(0, slots, widen, 0, unroll=4)

    def pick_all(n, out, first, count):
        def pick(k, _):
            for c, (lo, hi) in enumerate(spans):
                turned_s[n, k, :, lo:hi] = rows_s[c, pl.ds(k, slots, stride=images), :][:, 0 : hi - lo].astype(bf16)
            return 0

        lax.fori_loop(first, first + count, pick, 0)
        copy = pltpu.make_async_copy(turned_s.at[n, pl.ds(first, count)], out.at[pl.ds(first, count)], turn_sem.at[n])
        copy.start()
        return copy

    wide[...] = jnp.zeros_like(wide)
    part[...] = jnp.zeros_like(part)
    for copy in loads:
        copy.wait()
    wide[0:u, 0:w] = in_ot[...]
    wide[u : 2 * u, 0:w] = in_vt[...]
    for k in range(in_qk.shape[1] // w):
        wide[(k + 2) * u : (k + 3) * u, 0:w] = in_qk[:, k * w : (k + 1) * w]
    block[...] = wide[...].astype(bf16)
    part[0:6, 0:w] = in_vec[...]
    for r in range(in_upb.shape[1] // w):
        part[6 + r : 7 + r, 0:w] = in_upb[:, r * w : (r + 1) * w]

    greet(peers)
    gatherer = Gatherer(here, rows, block, all_ref, send, recv)
    gatherer.event(0)
    own_copy = pltpu.make_async_copy(block, all_ref.at[me[0], me[1]], local.at[0])
    own_copy.start()
    small_copy = pltpu.make_async_copy(part, small_ref.at[me[1]], local.at[1])
    small_copy.start()
    smalls = []
    for a in range(ys):
        for b in range(xs):
            if a or b:
                n = len(smalls)
                copy = pltpu.make_async_remote_copy(
                    src_ref=part,
                    dst_ref=small_ref.at[me[1]],
                    send_sem=small_send.at[n],
                    recv_sem=small_recv.at[me[1]],
                    device_id=here.to(dy=a, dx=b),
                    device_id_type=MESH,
                )
                copy.start()
                smalls.append(copy)
    turns = []
    jobs = [
        lambda: widen_all(0),
        lambda: turns.append(pick_all(0, tok_out, 0, images)),
        lambda: widen_all(1),
        lambda: turns.append(pick_all(1, cot_out, 0, images)),
    ]
    for t in range(1, gatherer.events()):
        if jobs:
            jobs.pop(0)()
        gatherer.event(t)
    for job in jobs:
        job()
    for a in range(ys):
        for b in range(xs):
            if a or b:
                peer = here.to(dy=a, dx=b)
                pltpu.make_async_remote_copy(
                    src_ref=part,
                    dst_ref=small_ref.at[peer[1]],
                    send_sem=small_send.at[0],
                    recv_sem=small_recv.at[peer[1]],
                    device_id=me,
                    device_id_type=MESH,
                ).wait_recv()
    gatherer.finish()
    for copy in smalls:
        copy.wait_send()
    own_copy.wait()
    small_copy.wait()
    for copy in turns:
        copy.wait()


def shape_of(dp, fsdp):
    cores = 2 if dp % 2 == 0 else 1
    ys = max(v for v in range(1, fsdp + 1) if fsdp % v == 0 and v * v <= fsdp)
    return dp // cores, ys, fsdp // ys, cores


def gather_all(dp, fsdp, rows, qk, vt, ot, vectors, up_bias, tokens, cotangent):
    images, slots, d = tokens.shape
    flat_bias = up_bias.reshape(1, -1)
    shards = (qk, vt, ot, vectors, flat_bias)
    return pl.pallas_call(
        partial(gather_kernel, dp, fsdp, rows),
        out_shape=[
            jax.ShapeDtypeStruct((dp, fsdp, rows, 128), bf16),
            jax.ShapeDtypeStruct((fsdp, 16, 128), f32),
            jax.ShapeDtypeStruct((images, slots, d), bf16),
            jax.ShapeDtypeStruct((images, slots, d), bf16),
        ],
        in_specs=[pl.BlockSpec(memory_space=pl.ANY)] * 7,
        out_specs=[pl.BlockSpec(memory_space=pl.ANY)] * 4,
        scratch_shapes=[
            pltpu.VMEM((rows, 128), f32),
            pltpu.VMEM((rows, 128), bf16),
            pltpu.VMEM((16, 128), f32),
            pltpu.VMEM((2, slots, images, d), bf16),
            pltpu.VMEM((-(-d // 128), slots * images, 128), f32),
            pltpu.VMEM((2, images, slots, d), bf16),
            *[pltpu.VMEM(v.shape, f32) for v in shards],
            pltpu.SemaphoreType.DMA((len(shards),)),
            pltpu.SemaphoreType.DMA((len(gatherer_keys(*shape_of(dp, fsdp))),)),
            pltpu.SemaphoreType.DMA((dp * fsdp, 2)),
            pltpu.SemaphoreType.DMA((fsdp,)),
            pltpu.SemaphoreType.DMA((fsdp,)),
            pltpu.SemaphoreType.DMA((2,)),
            pltpu.SemaphoreType.DMA((2,)),
        ],
        compiler_params=pltpu.CompilerParams(collective_id=0, has_side_effects=True, vmem_limit_bytes=62 * 1024 * 1024),
    )(*shards, tokens.transpose(1, 0, 2), cotangent.transpose(1, 0, 2))


def identity():
    rows = lax.broadcasted_iota(jnp.int32, (PITCH, PITCH), 0)
    cols = lax.broadcasted_iota(jnp.int32, (PITCH, PITCH), 1)
    return jnp.where(rows == cols, 1.0, 0.0).astype(bf16)


def one_hot(shape, w, goal):
    r = lax.broadcasted_iota(jnp.int32, shape, 0)
    c = lax.broadcasted_iota(jnp.int32, shape, 1)
    block, lane = r // 128, r % 128
    return jnp.where((c == goal(block, lane)) & (lane < w), 1.0, 0.0).astype(bf16)


def offset_planes(keys):
    j = lax.broadcasted_iota(jnp.int32, (keys, PITCH), 0)
    i = lax.broadcasted_iota(jnp.int32, (keys, PITCH), 1)
    rj, ri = j // GRID, i // GRID
    dc = ((j - rj * GRID) - (i - ri * GRID)).astype(f32)
    dr = (rj - ri).astype(f32)
    return dc, dr, dc * dc + dr * dr


def gates(locality_ref, heads):
    sig, cosig = [], []
    for h in range(heads):
        s = 1.0 / (1.0 + jnp.exp(-jnp.full((1, PITCH), locality_ref[3, h], f32)))
        sig.append(s)
        cosig.append(1.0 - s)
    return sig, cosig


def windows(heads, hw, d):
    wins = []
    for h in range(heads):
        lo = (h * hw) // 128 * 128
        wins.append((lo, min(lo + PITCH, d), h * hw - lo))
    return wins


def lane_sums(v):
    ones = jnp.ones((16, v.shape[1]), bf16)
    high = v.astype(bf16)
    low = (v - high.astype(f32)).astype(bf16)
    return (mm_nt(ones, high) + mm_nt(ones, low))[0:1]


def column(row):
    return jnp.broadcast_to(row, (128, 128)).T


def norm_stats(x):
    d = x.shape[0]
    mean = jnp.sum(x, axis=0, keepdims=True) * (1.0 / d)
    center = x - mean
    rstd = lax.rsqrt(jnp.sum(center * center, axis=0, keepdims=True) * (1.0 / d) + norm_eps)
    return center * rstd, rstd


def norm_back(grad, gain, normal, rstd):
    d = grad.shape[0]
    pull = grad * gain
    m1 = jnp.sum(pull, axis=0, keepdims=True) * (1.0 / d)
    m2 = jnp.sum(pull * normal, axis=0, keepdims=True) * (1.0 / d)
    return rstd * (pull - m1 - normal * m2)


def turn_in(ref, b, eye, pad_in, out):
    _, slots, d = ref.shape
    pad_in[0:slots, 0:d] = ref[b]
    for lo in range(0, d, PITCH):
        hi = min(lo + PITCH, d)
        out[lo:hi, :] = mm_nt(eye[0 : hi - lo, 0 : hi - lo], pad_in[:, lo:hi]).astype(bf16)


def turned(eye, ref, out_ref, row=0):
    for lo in range(0, ref.shape[1], PITCH):
        hi = min(lo + PITCH, ref.shape[1])
        out_ref[row + lo : row + hi, :] = mm_nt(eye[0 : hi - lo, 0 : hi - lo], ref[:, lo:hi]).astype(bf16)


def attend_kernel(
    images,
    slots,
    heads,
    dp,
    fsdp,
    total_steps,
    locality_ref,
    tok_ref,
    vis_ref,
    all_ref,
    small_ref,
    upt_ref,
    dn_ref,
    xt_ref,
    qkvt_ref,
    pa_ref,
    pb_ref,
    mixture_ref,
    wqk_ref,
    wv_ref,
    feed_ref,
    eye,
    pick,
    spread_a,
    spread_b,
    cat_s,
    chunk_s,
    whole_s,
    wide,
    block,
    wqkvt_s,
    vec_s,
    pad_in,
    placed,
    hid_s,
    kn_s,
    win_s,
    sc_s,
    mix_s,
    chunk_sem,
    own_sem,
    send,
    recv,
):
    d = tok_ref.shape[-1]
    u, w = d // dp, d // fsdp
    fu = upt_ref.shape[0]
    ring = chunk_s.shape[0]
    hw = d // heads
    keys = placed.shape[1]
    n = images * PITCH
    scale = hw**-0.5
    step = pl.program_id(0)
    here = Place(dp, fsdp)
    zs, ys, xs, cores = here.zs, here.ys, here.xs, here.cores
    me = here.to()
    gatherer = Gatherer(here, block.shape[0], block, feed_ref, send, recv)
    own_copy = pltpu.make_async_copy(block, feed_ref.at[me[0], me[1]], own_sem.at[0])

    @pl.when(step == 0)
    def _():
        def fetch(k):
            return pltpu.make_async_copy(all_ref.at[k], chunk_s.at[k % ring], chunk_sem.at[k % ring])

        for k in range(ring):
            fetch(k).start()
        wide[...] = jnp.zeros_like(wide)
        wide[0:fu, 0:w] = upt_ref[...]
        wide[up16(fu) : up16(fu) + fu, 0:w] = dn_ref[...]
        block[...] = wide[...].astype(bf16)
        peers = [here.to(dz=k) for k in range(1, zs)] + [here.to(dc=k) for k in range(1, cores)]
        peers += [here.to(dy=k) for k in range(1, ys)] + [here.to(dx=k) for k in range(1, xs)]
        greet(peers)
        gatherer.event(0)
        own_copy.start()

        eye[...] = identity()
        pad_in[...] = jnp.zeros_like(pad_in)
        dc, dr, far = offset_planes(keys)
        for h in range(heads):
            placed[h] = (locality_ref[0, h] * dc + locality_ref[1, h] * dr + locality_ref[2, h] * far) * LOG2E
        pick[...] = one_hot(pick.shape, w, lambda block, lane: block * w + lane)
        goal = lax.broadcasted_iota(jnp.int32, (d, 1), 0)
        goal = goal // w * (2 * w) + goal % w
        lane = lax.broadcasted_iota(jnp.int32, spread_a.shape, 1)
        spread_a[...] = jnp.where(lane == goal, 1.0, 0.0).astype(bf16)
        spread_b[...] = jnp.where(lane == goal + w, 1.0, 0.0).astype(bf16)

        for k in range(dp):
            fetch(k).wait()
            for f in range(fsdp):
                cat_s[:, 128 * f : 128 * (f + 1)] = chunk_s[k % ring, f].astype(f32)
            if k + ring < dp:
                fetch(k + ring).start()
            for p in range(3):
                whole_s[p, u * k : u * (k + 1), :] = cat_s[(p + 1) * u : (p + 2) * u, :]

        def dense(p):
            return mm(whole_s[p].astype(bf16), pick[...]).astype(bf16)

        wqkvt_s[2 * d : 3 * d, :] = dense(0)
        turned(eye, wqkvt_s.at[2 * d : 3 * d], wv_ref)
        joint = mm(dense(1), spread_a[...]) + mm(dense(2), spread_b[...])
        wqk_ref[0] = joint[:, 0:d].astype(bf16)
        wqk_ref[1] = joint[:, d : 2 * d].astype(bf16)
        turned(eye, wqk_ref.at[0], wqkvt_s)
        turned(eye, wqk_ref.at[1], wqkvt_s, d)
        for f in range(fsdp):
            for r in range(2):
                vec_s[r, w * f : w * (f + 1), :] = column(small_ref[f, r : r + 1, :])[0:w]
        for ref in (win_s, mix_s):
            ref[...] = jnp.zeros_like(ref)

    for t in range(1, gatherer.events()):

        @pl.when(step == min(t, total_steps - 1))
        def _(t=t):
            gatherer.event(t)

    def enter(b, _):
        turn_in(tok_ref, b, eye, pad_in, xt_ref.at[b])
        return 0

    lax.fori_loop(0, images, enter, 0)

    for t in range(n // 128):
        at = 128 * t
        normal, _ = norm_stats(xt_ref[at // PITCH, :, at % PITCH : at % PITCH + 128].astype(f32))
        hid_s[:, at : at + 128] = (normal * vec_s[0] + vec_s[1]).astype(bf16)
    joint = mm(wqkvt_s[...], hid_s[...]).astype(bf16)
    for b in range(images):
        qkvt_ref[b] = joint[:, PITCH * b : PITCH * (b + 1)]

    sig, cosig = gates(locality_ref, heads)
    wins = windows(heads, hw, d)

    def forward(b, _):
        kn_s[...] = mm_nt(eye[0:keys, :], qkvt_ref[b, d : 2 * d, :]).astype(bf16)
        key_vis = mm_nt(eye[0:keys, :], jnp.broadcast_to(vis_ref[b, 0:1, :], (PITCH, PITCH)).astype(bf16))
        bias = jnp.where(key_vis > 0.5, 0.0, -1e30)

        def fa(h):
            lo, hi, at = wins[h]
            win_s[h, at : at + hw, :] = qkvt_ref[b, h * hw : (h + 1) * hw, :]
            sc_s[h % 2] = mm(kn_s[:, lo:hi], win_s[h, 0 : hi - lo, :])

        def fb(h):
            scores = sc_s[h % 2] * (scale * LOG2E) + bias
            p = jnp.exp2(scores - jnp.max(scores, axis=0, keepdims=True))
            pa = p * (cosig[h] / jnp.sum(p, axis=0, keepdims=True))
            z = placed[h] + bias
            e = jnp.exp2(z - jnp.max(z, axis=0, keepdims=True))
            pb = e * (sig[h] / jnp.sum(e, axis=0, keepdims=True))
            pa_ref[b, h] = pa.astype(bf16)
            pb_ref[b, h] = pb.astype(bf16)
            mix_s[h, 0:keys, :] = (pa + pb).astype(bf16)

        def fc(h):
            mixture_ref[b, h * hw : (h + 1) * hw, :] = mm(
                qkvt_ref[b, 2 * d + h * hw : 2 * d + (h + 1) * hw, :], mix_s[h]
            ).astype(bf16)

        for t in range(heads + 2):
            if t < heads:
                fa(t)
            if t >= 2:
                fc(t - 2)
            if 1 <= t <= heads:
                fb(t - 1)
        return 0

    lax.fori_loop(0, images, forward, 0)

    @pl.when(step == total_steps - 1)
    def _():
        own_copy.wait()
        gatherer.finish()


def run_attend(dp, fsdp, tokens, vis, everything, small, upt, dn, locality, images):
    b, slots, d = tokens.shape
    heads = locality.shape[1]
    keys = up16(slots)
    n = images * PITCH
    u = d // dp
    rows = everything.shape[2]
    ring = dp if fsdp <= 4 else 2
    feed_rows = 2 * up16(upt.shape[0])

    def whole(shape):
        return pl.BlockSpec(shape, lambda g: (0,) * len(shape), pipeline_mode=pl.Buffered(1))

    def per(shape):
        return pl.BlockSpec((images,) + shape, lambda g: (g,) + (0,) * len(shape))

    kept_shapes = [(d, PITCH), (3 * d, PITCH), (heads, keys, PITCH), (heads, keys, PITCH), (d, PITCH)]
    scratch = [
        ((PITCH, PITCH), bf16),
        ((fsdp * 128, d), bf16),
        ((d, 2 * d), bf16),
        ((d, 2 * d), bf16),
        ((rows, fsdp * 128), f32),
        ((ring, fsdp, rows, 128), bf16),
        ((3, d, fsdp * 128), f32),
        ((feed_rows, 128), f32),
        ((feed_rows, 128), bf16),
        ((3 * d, d), bf16),
        ((2, d, 128), f32),
        ((PITCH, d), bf16),
        ((heads, keys, PITCH), f32),
        ((d, n), bf16),
        ((keys, d), bf16),
        ((heads, PITCH, PITCH), bf16),
        ((2, keys, PITCH), f32),
        ((heads, PITCH, PITCH), bf16),
    ]
    outs = pl.pallas_call(
        partial(attend_kernel, images, slots, heads, dp, fsdp, b // images),
        grid=(b // images,),
        out_shape=[jax.ShapeDtypeStruct((b,) + shape, bf16) for shape in kept_shapes]
        + [
            jax.ShapeDtypeStruct((2, d, d), bf16),
            jax.ShapeDtypeStruct((d, d), bf16),
            jax.ShapeDtypeStruct((dp, fsdp, feed_rows, 128), bf16),
        ],
        in_specs=[
            pl.BlockSpec(memory_space=pltpu.SMEM),
            per((slots, d)),
            per((1, PITCH)),
            pl.BlockSpec(memory_space=pl.ANY),
            whole(small.shape),
            whole(upt.shape),
            whole(dn.shape),
        ],
        out_specs=[per(shape) for shape in kept_shapes]
        + [whole((2, d, d)), whole((d, d)), pl.BlockSpec(memory_space=pl.ANY)],
        scratch_shapes=[pltpu.VMEM(*entry) for entry in scratch]
        + [
            pltpu.SemaphoreType.DMA((ring,)),
            pltpu.SemaphoreType.DMA((1,)),
            pltpu.SemaphoreType.DMA((len(gatherer_keys(*shape_of(dp, fsdp))),)),
            pltpu.SemaphoreType.DMA((dp * fsdp, 2)),
        ],
        compiler_params=pltpu.CompilerParams(
            dimension_semantics=("arbitrary",),
            collective_id=2,
            has_side_effects=True,
            vmem_limit_bytes=62 * 1024 * 1024,
        ),
        cost_estimate=pl.CostEstimate(flops=20_000_000_000, bytes_accessed=70_000_000, transcendentals=0),
    )(locality, tokens, vis, everything, small, upt, dn)
    return outs


def feed_kernel(
    images,
    slots,
    cot_ref,
    vis_ref,
    xt_ref,
    mixture_ref,
    all_ref,
    feed_ref,
    small_ref,
    res_ref,
    dot_ref,
    mg_ref,
    part_ref,
    gsmall_ref,
    eye,
    pick,
    chunk_s,
    chunk_sem,
    o_s,
    wot_s,
    wo_s,
    wupt_s,
    wup_s,
    wdnt_s,
    wdn_s,
    vec_s,
    upb_s,
    pad_in,
    acc_out,
    acc_up,
    acc_down,
    acc_vec,
    acc_upb,
    mixture_s,
    xh2_s,
    rstd_s,
    second_s,
    mid_s,
    cot_s,
    dlow_s,
    up_s,
    back_s,
    act_s,
    ug_s,
    blow_s,
):
    d = cot_ref.shape[-1]
    ff = upb_s.shape[0]
    dp, fsdp, o_at, _ = feed_ref.shape
    u, w = d // dp, d // fsdp
    fu = ff // dp
    dn_at = up16(fu)
    ring = chunk_s.shape[0]
    fits = ring == dp
    split = row_plan(fu, u)[1]
    few = o_s.shape[2]
    n = images * PITCH
    step = pl.program_id(0)

    @pl.when(step == 0)
    def _():
        def fetch(k):
            return pltpu.make_async_copy(
                feed_ref.at[k], chunk_s.at[k % ring, :, pl.ds(0, o_at)], chunk_sem.at[k % ring]
            )

        for k in range(ring):
            fetch(k).start()
        rest = pltpu.make_async_copy(all_ref.at[:, :, pl.ds(0, few)], o_s, chunk_sem.at[ring])
        rest.start()
        eye[...] = identity()
        pad_in[...] = jnp.zeros_like(pad_in)
        pick[...] = one_hot(pick.shape, w, lambda block, lane: block * w + lane)

        def unpack(k, _):
            fetch(k).wait()


            def joined(at):
                return jnp.concatenate([chunk_s[k % ring, f, at : at + fu] for f in range(fsdp)], axis=1)

            big = slice(fu * k, fu * (k + 1))
            acc_up[big, :] = mm(joined(0), pick[...])
            acc_down[big, :] = mm(joined(dn_at), pick[...])
            if k + ring < dp:
                fetch(k + ring).start()
            return 0

        if fits:
            for k in range(dp):
                fetch(k).wait()
                for f in range(fsdp):
                    act_s[fu * k : fu * (k + 1), 128 * f : 128 * (f + 1)] = chunk_s[k, f, 0:fu]
                    ug_s[fu * k : fu * (k + 1), 128 * f : 128 * (f + 1)] = chunk_s[k, f, dn_at : dn_at + fu]
            wupt_s[...] = mm(act_s[...], pick[...]).astype(bf16)
            wdn_s[...] = mm(ug_s[...], pick[...]).astype(bf16)
        else:
            for k in range(dp):
                unpack(k, 0)
            wupt_s[...] = acc_up[...].astype(bf16)
            wdn_s[...] = acc_down[...].astype(bf16)
        turned(eye, wupt_s, wup_s)
        turned(eye, wdn_s, wdnt_s)
        rest.wait()
        for k in range(dp):
            joined = jnp.concatenate([o_s[k, f, 0:u] for f in range(fsdp)], axis=1)
            if fits:
                mid_s[u * k : u * (k + 1), :] = joined.astype(f32)
            else:
                acc_out[u * k : u * (k + 1), :] = mm(joined, pick[...])
        wot_s[...] = (mm(mid_s[...].astype(bf16), pick[...]) if fits else acc_out[...]).astype(bf16)
        turned(eye, wot_s, wo_s)
        for f in range(fsdp):
            for r in range(2, 6):
                vec_s[r, w * f : w * (f + 1), :] = column(small_ref[f, r : r + 1, :])[0:w]
            for r in range(ff // d):
                at = (f * (ff // d) + r) * w
                upb_s[at : at + w, :] = column(small_ref[f, 6 + r : 7 + r, :])[0:w]
        for ref in (acc_out, acc_up, acc_down, acc_vec, acc_upb):
            ref[...] = jnp.zeros_like(ref)

    tiles = [slice(128 * k, 128 * (k + 1)) for k in range(n // 128)]

    def seen(t):
        at = 128 * t
        return vis_ref[at // PITCH, 0:1, at % PITCH : at % PITCH + 128]

    def fold(v):
        total = v[:, 0:128]
        for k in range(1, n // 128):
            total = total + v[:, 128 * k : 128 * (k + 1)]
        return total

    def enter(b, _):
        cols = pl.ds(pl.multiple_of(b * PITCH, PITCH), PITCH)
        turn_in(cot_ref, b, eye, pad_in, cot_s.at[:, cols])
        mixture_s[:, cols] = mixture_ref[b]
        return 0

    lax.fori_loop(0, images, enter, 0)

    def x_tile(t):
        at = 128 * t
        return xt_ref[at // PITCH, :, at % PITCH : at % PITCH + 128].astype(f32)

    for t, tile in enumerate(tiles):
        down = cot_s[:, tile].astype(f32) * seen(t)
        dlow_s[:, tile] = down.astype(bf16)
        acc_vec[3] += down
    mid_s[...] = mm(wot_s[...], mixture_s[...])
    for t, tile in enumerate(tiles):
        middle = x_tile(t) + seen(t) * (mid_s[:, tile] + vec_s[4])
        mid_s[:, tile] = middle
        normal, rstd = norm_stats(middle)
        xh2_s[:, tile] = normal
        rstd_s[0:1, tile] = rstd
        second_s[:, tile] = (normal * vec_s[2] + vec_s[3]).astype(bf16)

    chunk = up_s.shape[1]
    steps = ff // chunk

    def feed_start(c):
        part = slice(c * chunk, (c + 1) * chunk)
        up_s[c % 2] = mm(wupt_s[part, :], second_s[...])
        back_s[c % 2] = mm(wdn_s[part, :], dlow_s[...])

    feed_start(0)
    for c in range(steps):
        if c + 1 < steps:
            feed_start(c + 1)
        part = slice(c * chunk, (c + 1) * chunk)
        act, slope = gelu_parts(up_s[c % 2] + jnp.concatenate([upb_s[part, :]] * (n // 128), axis=1))
        act_s[part, :] = act.astype(bf16)
        ug = (back_s[c % 2] * slope).astype(bf16)
        ug_s[part, :] = ug
        acc_upb[part, :] += fold(ug.astype(f32))

    second_grad = mm(wup_s[...], ug_s[...])
    acc_up[...] += mm_nt(ug_s[...], second_s[...])
    for t, tile in enumerate(tiles):
        grad = second_grad[:, tile]
        normal = xh2_s[:, tile]
        acc_vec[0] += grad * normal
        acc_vec[1] += grad
        middle_grad = cot_s[:, tile].astype(f32) + norm_back(grad, vec_s[2], normal, rstd_s[0:1, tile])
        at = 128 * t
        mg_ref[at // PITCH, :, at % PITCH : at % PITCH + 128] = middle_grad.astype(bf16)
        low = (seen(t) * middle_grad).astype(bf16)
        blow_s[:, tile] = low
        acc_vec[2] += low.astype(f32)
    acc_down[...] += mm_nt(act_s[...], dlow_s[...])
    mixture_grad = mm(wo_s[...], blow_s[...]).astype(bf16)
    for b in range(images):
        dot_ref[b] = mixture_grad[:, PITCH * b : PITCH * (b + 1)]
    acc_out[...] += mm_nt(blow_s[...], mixture_s[...])
    downward = mm(wdnt_s[...], act_s[...])
    for t, tile in enumerate(tiles):
        dlow_s[:, tile] = (mid_s[:, tile] + seen(t) * (downward[:, tile] + vec_s[5])).astype(bf16)
    for b in range(images):
        res_ref[b] = mm_nt(eye[0:slots, :], dlow_s[:, b * PITCH : (b + 1) * PITCH]).astype(bf16)

    @pl.when(step == pl.num_programs(0) - 1)
    def _():
        def put_rest(k):
            return pltpu.make_async_copy(
                chunk_s.at[k % 2, :, pl.ds(0, split - o_at)],
                part_ref.at[k, :, pl.ds(o_at, split - o_at)],
                chunk_sem.at[k % 2],
            )

        chunk_s[...] = jnp.zeros_like(chunk_s)
        for k in [] if fits else range(dp):
            piece = mm_nt(acc_out[u * k : u * (k + 1), :].astype(bf16), pick[...]).astype(bf16)
            if k >= 2:
                put_rest(k - 2).wait()
            for f in range(fsdp):
                chunk_s[k % 2, f, 0:u] = piece[:, 128 * f : 128 * (f + 1)]
            put_rest(k).start()
        for k in [] if fits else range(max(dp - 2, 0), dp):
            put_rest(k).wait()
        def put(k):
            if fits:
                return pltpu.make_async_copy(chunk_s.at[k], part_ref.at[k], chunk_sem.at[k])
            return pltpu.make_async_copy(
                chunk_s.at[k % 2, :, pl.ds(0, o_at)], part_ref.at[k, :, pl.ds(0, o_at)], chunk_sem.at[k % 2]
            )

        def pack(k, _):
            big = slice(fu * k, fu * (k + 1))

            if k >= 2:
                put(k - 2).wait()

            for at, ref in ((0, acc_up), (dn_at, acc_down)):
                piece = mm_nt(ref[big, :].astype(bf16), pick[...]).astype(bf16)
                for f in range(fsdp):
                    chunk_s[k % 2, f, at : at + fu] = piece[:, 128 * f : 128 * (f + 1)]
            put(k).start()
            return 0

        if fits:
            act_s[...] = mm_nt(acc_up[...].astype(bf16), pick[...]).astype(bf16)
            ug_s[...] = mm_nt(acc_down[...].astype(bf16), pick[...]).astype(bf16)
            mid_s[...] = mm_nt(acc_out[...].astype(bf16), pick[...])
            for k in range(dp):
                for f in range(fsdp):
                    lane = slice(128 * f, 128 * (f + 1))
                    chunk_s[k, f, 0:fu] = act_s[fu * k : fu * (k + 1), lane]
                    chunk_s[k, f, dn_at : dn_at + fu] = ug_s[fu * k : fu * (k + 1), lane]
                    chunk_s[k, f, o_at : o_at + u] = mid_s[u * k : u * (k + 1), lane].astype(bf16)
                put(k).start()
        else:
            for k in range(dp):
                pack(k, 0)
        for k in range(0 if fits else max(dp - 2, 0), dp):
            put(k).wait()

        gsmall_ref[...] = jnp.zeros_like(gsmall_ref)
        for f in range(fsdp):
            for r in range(4):
                gsmall_ref[f, 2 + r : 3 + r, 0:w] = lane_sums(acc_vec[r, w * f : w * (f + 1), :])
            for r in range(ff // d):
                lo = (f * (ff // d) + r) * w
                gsmall_ref[f, 6 + r : 7 + r, 0:w] = lane_sums(acc_upb[lo : lo + w, :])


def run_feed(dp, fsdp, cotangent, vis, xt, mixture, everything, feed, small, ff, images):
    b, slots, d = cotangent.shape
    n = images * PITCH
    o_at, split, _ = row_plan(ff // dp, d // dp)
    few = up16(d // dp)
    ring = dp if n == fsdp * 128 else 2

    def whole(shape):
        return pl.BlockSpec(shape, lambda g: (0,) * len(shape), pipeline_mode=pl.Buffered(1))

    def per(shape):
        return pl.BlockSpec((images,) + shape, lambda g: (g,) + (0,) * len(shape))

    scratch = [
        ((PITCH, PITCH), bf16),
        ((fsdp * 128, d), bf16),
        ((ring, fsdp, split if ring == dp else o_at, 128), bf16),
        None,
        ((dp, fsdp, few, 128), bf16),
        ((d, d), bf16),
        ((d, d), bf16),
        ((ff, d), bf16),
        ((d, ff), bf16),
        ((d, ff), bf16),
        ((ff, d), bf16),
        ((6, d, 128), f32),
        ((ff, 128), f32),
        ((PITCH, d), bf16),
        ((d, d), f32),
        ((ff, d), f32),
        ((ff, d), f32),
        ((4, d, 128), f32),
        ((ff, 128), f32),
        ((d, n), bf16),
        ((d, n), f32),
        ((8, n), f32),
        ((d, n), bf16),
        ((d, n), f32),
        ((d, n), bf16),
        ((d, n), bf16),
        ((2, ff // 6, n), f32),
        ((2, ff // 6, n), f32),
        ((ff, n), bf16),
        ((ff, n), bf16),
        ((d, n), bf16),
    ]
    scratch = [pltpu.SemaphoreType.DMA((ring + 1,)) if entry is None else pltpu.VMEM(*entry) for entry in scratch]
    return pl.pallas_call(
        partial(feed_kernel, images, slots),
        grid=(b // images,),
        out_shape=[
            jax.ShapeDtypeStruct((b, slots, d), bf16),
            jax.ShapeDtypeStruct((b, d, PITCH), bf16),
            jax.ShapeDtypeStruct((b, d, PITCH), bf16),
            jax.ShapeDtypeStruct((dp, fsdp, split, 128), bf16),
            jax.ShapeDtypeStruct((fsdp, 16, 128), f32),
        ],
        in_specs=[per((slots, d)), per((1, PITCH)), per((d, PITCH)), per((d, PITCH))]
        + [pl.BlockSpec(memory_space=pl.ANY)] * 2
        + [whole((fsdp, 16, 128))],
        out_specs=[per((slots, d)), per((d, PITCH)), per((d, PITCH)), pl.BlockSpec(memory_space=pl.ANY), whole((fsdp, 16, 128))],
        scratch_shapes=scratch,
        compiler_params=pltpu.CompilerParams(
            dimension_semantics=("arbitrary",), vmem_limit_bytes=63 * 1024 * 1024
        ),
        cost_estimate=pl.CostEstimate(flops=40_000_000_000, bytes_accessed=40_000_000, transcendentals=0),
    )(cotangent, vis, xt, mixture, everything, feed, small)


class Reducer:
    def __init__(self, here, rows, mine, theirs, other, bufs, send, recv):
        self.here, self.mine, self.theirs, self.other = here, mine, theirs, other
        self.got_x, self.got_y, self.got_x2, self.got_y2, self.got_z = bufs
        self.send, self.recv = send, recv
        half = rows // 32 * 16
        self.segs = (pl.ds(0, half), pl.ds(half, rows - half))
        self.order = z_order(here.zs)
        self.keys = reducer_keys(here.zs, here.ys, here.xs, here.cores)

    def f_at(self, dy, dx):
        return self.here.to(dy=dy, dx=dx)[1]

    def copy(self, key):
        here, segs, n = self.here, self.segs, key[1]
        if key[0] == "pair":
            src, dst, target = self.theirs(n), self.other.at[n], here.to(dc=1)
        elif key[0] == "a1":
            _, _, a, b = key
            src, dst, target = self.mine(n).at[self.f_at(a, b), segs[0]], self.got_x.at[n, a, b - 1], here.to(dx=b)
        elif key[0] == "b1":
            _, _, a, b = key
            src, dst, target = self.mine(n).at[self.f_at(a, b), segs[1]], self.got_y.at[n, b, a - 1], here.to(dy=a)
        elif key[0] == "a2":
            src, dst, target = self.mine(n).at[self.f_at(key[2], 0), segs[0]], self.got_y2.at[n, key[2] - 1], here.to(dy=key[2])
        elif key[0] == "b2":
            src, dst, target = self.mine(n).at[self.f_at(0, key[2]), segs[1]], self.got_x2.at[n, key[2] - 1], here.to(dx=key[2])
        else:
            seg = segs[key[2]]
            src, dst, target = self.mine(n).at[self.f_at(0, 0), seg], self.got_z.at[n, seg], here.to(dz=self.order[n])
        at = self.keys.index(key)
        return pltpu.make_async_remote_copy(
            src_ref=src, dst_ref=dst, send_sem=self.send.at[at], recv_sem=self.recv.at[at], device_id=target, device_id_type=MESH
        )

    def add(self, n, f, seg, got):
        ref = self.mine(n)
        ref[f, self.segs[seg]] = (ref[f, self.segs[seg]].astype(f32) + got.astype(f32)).astype(bf16)

    def begin(self):
        if self.here.cores > 1:
            for n in range(self.here.zs):
                self.copy(("pair", n)).start()

    def stage_one(self, n):
        here = self.here
        if here.cores > 1:
            self.copy(("pair", n)).wait_recv()
            ref = self.mine(n)

            def body(f, _):
                ref[f] = (ref[f].astype(f32) + self.other[n, f].astype(f32)).astype(bf16)
                return 0

            lax.fori_loop(0, here.fs, body, 0)
        for a in list(range(1, here.ys)) + [0]:
            for b in range(1, here.xs):
                self.copy(("a1", n, a, b)).start()
        for b in list(range(1, here.xs)) + [0]:
            for a in range(1, here.ys):
                self.copy(("b1", n, a, b)).start()

    def stage_two(self, n):
        here = self.here
        for a in list(range(1, here.ys)) + [0]:
            for b in range(1, here.xs):
                self.copy(("a1", n, a, b)).wait_recv()
                self.add(n, self.f_at(a, 0), 0, self.got_x[n, a, b - 1])
            if a:
                self.copy(("a2", n, a)).start()
        for b in list(range(1, here.xs)) + [0]:
            for a in range(1, here.ys):
                self.copy(("b1", n, a, b)).wait_recv()
                self.add(n, self.f_at(0, b), 1, self.got_y[n, b, a - 1])
            if b:
                self.copy(("b2", n, b)).start()

    def stage_three(self, n):
        here = self.here
        for a in range(1, here.ys):
            self.copy(("a2", n, a)).wait_recv()
            self.add(n, self.f_at(0, 0), 0, self.got_y2[n, a - 1])
        for b in range(1, here.xs):
            self.copy(("b2", n, b)).wait_recv()
            self.add(n, self.f_at(0, 0), 1, self.got_x2[n, b - 1])
        if self.order[n]:
            for seg in (0, 1):
                self.copy(("z", n, seg)).start()

    def turn(self, t):
        zs = self.here.zs
        if t < zs:
            self.stage_one(t)
        if 1 <= t <= zs:
            self.stage_two(t - 1)
        if 2 <= t < zs + 2:
            self.stage_three(t - 2)

    def total(self):
        zs = self.here.zs
        total = self.mine(zs - 1)[self.f_at(0, 0)].astype(f32)
        for n in range(zs - 1):
            for seg in (0, 1):
                self.copy(("z", n, seg)).wait_recv()
            total = total + self.got_z[n].astype(f32)
        return total

    def finish(self):
        for key in self.keys:
            self.copy(key).wait_send()


def z_order(zs):
    return sorted(range(1, zs), key=lambda k: min(k, zs - k)) + [0]


def reducer_keys(zs, ys, xs, cores):
    keys = []
    for n in range(zs):
        if cores > 1:
            keys.append(("pair", n))
        keys += [("a1", n, a, b) for a in range(ys) for b in range(1, xs)]
        keys += [("b1", n, a, b) for a in range(1, ys) for b in range(xs)]
        keys += [("a2", n, a) for a in range(1, ys)] + [("b2", n, b) for b in range(1, xs)]
        if n < zs - 1:
            keys += [("z", n, 0), ("z", n, 1)]
    return keys


def reducer_buffers(zs, ys, xs, rows):
    half = rows // 32 * 16
    rest = rows - half
    return [
        pltpu.VMEM((zs, ys, max(xs - 1, 1), half, 128), bf16),
        pltpu.VMEM((zs, xs, max(ys - 1, 1), rest, 128), bf16),
        pltpu.VMEM((zs, max(xs - 1, 1), rest, 128), bf16),
        pltpu.VMEM((zs, max(ys - 1, 1), half, 128), bf16),
        pltpu.VMEM((zs, rows, 128), bf16),
    ]


def exchange(here, ref, buf, send, recv, base, coordinate, size, targets):
    buf[base + coordinate] = ref[...]
    for k, target in enumerate(targets):
        pltpu.make_async_remote_copy(
            src_ref=ref,
            dst_ref=buf.at[base + coordinate],
            send_sem=send.at[base + k],
            recv_sem=recv.at[base + coordinate],
            device_id=target,
            device_id_type=MESH,
        ).start()

    def add():
        for k in range(1, size):
            pltpu.make_async_remote_copy(
                src_ref=ref,
                dst_ref=buf.at[base + coordinate],
                send_sem=send.at[base + k - 1],
                recv_sem=recv.at[base],
                device_id=here.to(),
                device_id_type=MESH,
            ).wait_send()
        for k in range(1, size):
            at = base + lax.rem(coordinate + k, size)
            pltpu.make_async_remote_copy(
                src_ref=ref,
                dst_ref=buf.at[at],
                send_sem=send.at[base],
                recv_sem=recv.at[at],
                device_id=here.to(),
                device_id_type=MESH,
            ).wait_recv()
        total = buf[base]
        for k in range(1, size):
            total = total + buf[base + k]
        ref[...] = total

    return add


def backward_kernel(
    images,
    slots,
    heads,
    dp,
    fsdp,
    ff,
    total_steps,
    locality_ref,
    xt_ref,
    qkvt_ref,
    pa_ref,
    pb_ref,
    dot_ref,
    mg_ref,
    small_ref,
    gsmall_ref,
    wqk_ref,
    wv_ref,
    part_ref,
    tgrad_ref,
    grad_ref,
    sum_ref,
    norm_ref,
    eye,
    pick,
    perm,
    cat_s,
    whole_s,
    vec_s,
    acc_qk,
    acc_v,
    acc_vec,
    acc_place,
    acc_gate,
    hid_s,
    xh_s,
    rstd_s,
    vn_s,
    win_s,
    sc_s,
    mix_s,
    ds_s,
    dqkv_s,
    tg_s,
    last_s,
    a_mine,
    a_other,
    a_x,
    a_y,
    a_x2,
    a_y2,
    a_z,
    b_other,
    b_x,
    b_y,
    b_x2,
    b_y2,
    b_z,
    small_buf,
    norm_buf,
    load,
    a_send,
    a_recv,
    b_send,
    b_recv,
    sm_send,
    sm_recv,
    nm_send,
    nm_recv,
):
    d = xt_ref.shape[1]
    u, w = d // dp, d // fsdp
    _, split, rows_all = row_plan(ff // dp, u)
    hw = d // heads
    keys = acc_place.shape[1]
    n = images * PITCH
    scale = hw**-0.5
    fits = fsdp <= 4
    step = pl.program_id(0)
    count = pl.num_programs(0)
    here = Place(dp, fsdp)
    zs, ys, xs, cores = here.zs, here.ys, here.xs, here.cores
    order = z_order(zs)

    def plane(k, dc=0):
        return here.to(dz=order[k], dc=dc)[0]

    first = Reducer(
        here,
        split,
        lambda k: a_mine.at[k],
        lambda k: part_ref.at[plane(k, 1)],
        a_other,
        (a_x, a_y, a_x2, a_y2, a_z),
        a_send,
        a_recv,
    )
    last = Reducer(
        here,
        rows_all - split,
        lambda k: last_s.at[plane(k)],
        lambda k: last_s.at[plane(k, 1)],
        b_other,
        (b_x, b_y, b_x2, b_y2, b_z),
        b_send,
        b_recv,
    )

    def loading(k):
        return pltpu.make_async_copy(part_ref.at[plane(k)], a_mine.at[k], load.at[k])

    @pl.when(step == 0)
    def _():
        for k in range(zs):
            loading(k).start()
        peers = [here.to(dz=k) for k in range(1, zs)] + [here.to(dc=k) for k in range(1, cores)]
        peers += [here.to(dy=a, dx=b) for a in range(ys) for b in range(xs) if a or b]
        peers = [
            here.to(dz=k, dc=c, dy=a, dx=b)
            for k in range(zs)
            for c in range(cores)
            for a in range(ys)
            for b in range(xs)
            if k or c or a or b
        ]
        greet(peers)
        first.begin()
        eye[...] = identity()
        pick[...] = one_hot(pick.shape, w, lambda block, lane: block * w + lane)
        e = lax.broadcasted_iota(jnp.int32, (2 * d, 1), 0)
        goal = (e % (2 * w)) // w * d + e // (2 * w) * w + e % w
        perm[...] = jnp.where(lax.broadcasted_iota(jnp.int32, perm.shape, 1) == goal, 1.0, 0.0).astype(bf16)
        for f in range(fsdp):
            for r in range(2):
                vec_s[r, w * f : w * (f + 1), :] = column(small_ref[f, r : r + 1, :])[0:w]
        for ref in (acc_qk, acc_v, acc_vec, acc_place, acc_gate, win_s, mix_s, ds_s):
            ref[...] = jnp.zeros_like(ref)
        for k in range(zs):
            loading(k).wait()

    spread = total_steps
    for t in range(zs + 2):

        @pl.when(step == min(t + 1, spread - 1))
        def _(t=t):
            first.turn(t)

    sig, cosig = gates(locality_ref, heads)
    wins = windows(heads, hw, d)
    tiles = [slice(128 * k, 128 * (k + 1)) for k in range(n // 128)]

    def place_of(t):
        at = 128 * t
        return at // PITCH, slice(at % PITCH, at % PITCH + 128)

    for t, tile in enumerate(tiles):
        b, lane = place_of(t)
        normal, rstd = norm_stats(xt_ref[b, :, lane].astype(f32))
        xh_s[:, tile] = normal
        rstd_s[0:1, tile] = rstd
        hid_s[:, tile] = (normal * vec_s[0] + vec_s[1]).astype(bf16)

    def backward(b, _):
        cols = pl.ds(pl.multiple_of(b * PITCH, PITCH), PITCH)
        vn_s[...] = mm_nt(eye[0:keys, :], qkvt_ref[b, 2 * d : 3 * d, :]).astype(bf16)

        def ba(h):
            lo, hi, at = wins[h]
            win_s[h, at : at + hw, :] = dot_ref[b, h * hw : (h + 1) * hw, :]
            sc_s[h % 2] = mm(vn_s[:, lo:hi], win_s[h, 0 : hi - lo, :])

        def bb(h):
            g = sc_s[h % 2]
            pa = pa_ref[b, h].astype(f32)
            pb = pb_ref[b, h].astype(f32)
            mix_s[h, 0:keys, :] = pa_ref[b, h] + pb_ref[b, h]
            pull_a = jnp.sum(g * pa, axis=0, keepdims=True) / cosig[h]
            pull_b = jnp.sum(g * pb, axis=0, keepdims=True) / sig[h]
            acc_gate[h : h + 1, :] += pull_b - pull_a
            acc_place[h] += pb * (g - pull_b)
            ds_s[h, 0:keys, :] = (pa * (g - pull_a)).astype(bf16)

        def bc(h):
            rows = slice(h * hw, (h + 1) * hw)
            dqkv_s[rows, cols] = (mm(qkvt_ref[b, d + h * hw : d + (h + 1) * hw, :], ds_s[h]) * scale).astype(bf16)
            dqkv_s[d + h * hw : d + (h + 1) * hw, cols] = (mm_nt(qkvt_ref[b, rows, :], ds_s[h]) * scale).astype(bf16)
            dqkv_s[2 * d + h * hw : 2 * d + (h + 1) * hw, cols] = mm_nt(dot_ref[b, rows, :], mix_s[h]).astype(bf16)

        for t in range(heads + 2):
            if t < heads:
                ba(t)
            if t >= 2:
                bc(t - 2)
            if 1 <= t <= heads:
                bb(t - 1)
        return 0

    lax.fori_loop(0, images, backward, 0)

    back = mm(wqk_ref[0], dqkv_s[0:d, :]) + mm(wqk_ref[1], dqkv_s[d : 2 * d, :]) + mm(wv_ref[...], dqkv_s[2 * d : 3 * d, :])
    acc_qk[...] += mm_nt(hid_s[...], dqkv_s[0 : 2 * d, :])
    for t, tile in enumerate(tiles):
        b, lane = place_of(t)
        grad = back[:, tile]
        normal = xh_s[:, tile]
        acc_vec[0] += grad * normal
        acc_vec[1] += grad
        pulled = norm_back(grad, vec_s[0], normal, rstd_s[0:1, tile])
        tg_s[:, tile] = (mg_ref[b, :, lane].astype(f32) + pulled).astype(bf16)
    acc_v[...] += mm_nt(dqkv_s[2 * d : 3 * d, :], hid_s[...])
    for b in range(images):
        tgrad_ref[b] = mm_nt(eye[0:slots, :], tg_s[:, b * PITCH : (b + 1) * PITCH]).astype(bf16)

    @pl.when(step == count - 1)
    def _():
        cat_s[...] = jnp.zeros_like(cat_s)
        acc_qk[...] = mm(acc_qk[...].astype(bf16), perm[...])
        if fits:
            whole_s[0] = mm_nt(acc_v[...].astype(bf16), pick[...])
            whole_s[1] = mm_nt(acc_qk[:, 0:d].astype(bf16), pick[...])
            whole_s[2] = mm_nt(acc_qk[:, d : 2 * d].astype(bf16), pick[...])
        for k in range(dp):
            own = slice(u * k, u * (k + 1))
            if fits:
                for p in range(3):
                    cat_s[p * u : (p + 1) * u, :] = whole_s[p, own, :]
            else:
                cat_s[0:u, :] = mm_nt(acc_v[own, :].astype(bf16), pick[...])
                cat_s[u : 2 * u, :] = mm_nt(acc_qk[own, 0:d].astype(bf16), pick[...])
                cat_s[2 * u : 3 * u, :] = mm_nt(acc_qk[own, d : 2 * d].astype(bf16), pick[...])
            for f in range(fsdp):
                last_s[k, f] = cat_s[:, 128 * f : 128 * (f + 1)].astype(bf16)
        last.begin()

        sum_ref[...] = gsmall_ref[...]
        for f in range(fsdp):
            for r in range(2):
                sum_ref[f, r : r + 1, 0:w] = lane_sums(acc_vec[r, w * f : w * (f + 1), :])
        at = 6 + ff // d
        dc, dr, far = offset_planes(keys)
        rows = [[], [], []]
        for h in range(heads):
            pg = acc_place[h]
            for c, off in enumerate((dc, dr, far)):
                rows[c].append(jnp.sum(pg * off, axis=0, keepdims=True))
            acc_gate[h : h + 1, :] = acc_gate[h : h + 1, :] * (sig[h] * cosig[h])
        sum_ref[0, at + 3 : at + 4, 0 : acc_gate.shape[0]] = lane_sums(acc_gate[...])
        for c in range(3):
            for h in range(heads):
                acc_gate[h : h + 1, :] = rows[c][h]
            sum_ref[0, at + c : at + c + 1, 0 : acc_gate.shape[0]] = lane_sums(acc_gate[...])


        def small_round(base, coordinate, size, targets):
            return exchange(here, sum_ref, small_buf, sm_send, sm_recv, base, coordinate, size, targets)

        pending = small_round(0, here.c, cores, [here.to(dc=k) for k in range(1, cores)])
        total = first.total()
        grad_ref[0:split, :] = total
        squares = jnp.sum((total * total).reshape(split // 8, 8, 128), axis=0)
        for t in range(zs + 2):
            last.turn(t)
            if t == 0:
                pending()
                pending = small_round(cores, here.x, xs, [here.to(dx=b) for b in range(1, xs)])
            if t == 1:
                pending()
                pending = small_round(cores + xs, here.y, ys, [here.to(dy=a) for a in range(1, ys)])
            if t == 2:
                pending()
                pending = small_round(cores + xs + ys, here.z, zs, [here.to(dz=q) for q in range(1, zs)])
        pending()
        total = last.total()
        grad_ref[split:rows_all, :] = total
        norm_ref[...] = squares + jnp.sum((total * total).reshape((rows_all - split) // 8, 8, 128), axis=0)
        at = here.to()
        everyone = [
            here.to(dz=k, dc=c, dy=a, dx=b)
            for k in range(zs)
            for c in range(cores)
            for a in range(ys)
            for b in range(xs)
            if k or c or a or b
        ]
        exchange(here, norm_ref, norm_buf, nm_send, nm_recv, 0, at[0] * fsdp + at[1], dp * fsdp, everyone)()
        first.finish()
        last.finish()


def run_backward(dp, fsdp, slots, kept, small, small_part, wqk, wv, first_part, locality, ff, images):
    b, d, _ = kept[0].shape
    heads = locality.shape[1]
    keys = kept[2].shape[2]
    n = images * PITCH
    _, split, rows = row_plan(ff // dp, d // dp)
    more = rows - split
    cores = 2 if dp % 2 == 0 else 1
    zs = dp // cores
    ys = max(v for v in range(1, fsdp + 1) if fsdp % v == 0 and v * v <= fsdp)
    xs = fsdp // ys
    copies = len(reducer_keys(zs, ys, xs, cores))
    rounds = cores + xs + ys + zs

    def whole(shape):
        return pl.BlockSpec(shape, lambda g: (0,) * len(shape), pipeline_mode=pl.Buffered(1))

    def per(shape):
        mode = pl.Buffered(1) if fsdp > 4 and shape[-1] == PITCH else None
        return pl.BlockSpec((images,) + shape, lambda g: (g,) + (0,) * len(shape), pipeline_mode=mode)

    scratch = [
        pltpu.VMEM((PITCH, PITCH), bf16),
        pltpu.VMEM((fsdp * 128, d), bf16),
        pltpu.VMEM((2 * d, 2 * d), bf16),
        pltpu.VMEM((more, fsdp * 128), f32),
        pltpu.VMEM((3, d, fsdp * 128) if fsdp <= 4 else (1, 8, 128), f32),
        pltpu.VMEM((2, d, 128), f32),
        pltpu.VMEM((d, 2 * d), f32),
        pltpu.VMEM((d, d), f32),
        pltpu.VMEM((2, d, 128), f32),
        pltpu.VMEM((heads, keys, PITCH), f32),
        pltpu.VMEM((-(-heads // 8) * 8, PITCH), f32),
        pltpu.VMEM((d, n), bf16),
        pltpu.VMEM((d, n), f32),
        pltpu.VMEM((8, n), f32),
        pltpu.VMEM((keys, d), bf16),
        pltpu.VMEM((heads, PITCH, PITCH), bf16),
        pltpu.VMEM((2, keys, PITCH), f32),
        pltpu.VMEM((heads, PITCH, PITCH), bf16),
        pltpu.VMEM((heads, PITCH, PITCH), bf16),
        pltpu.VMEM((3 * d, n), bf16),
        pltpu.VMEM((d, n), bf16),
        pltpu.VMEM((dp, fsdp, more, 128), bf16),
        pltpu.VMEM((zs, fsdp, split, 128), bf16),
        pltpu.VMEM((zs, fsdp, split, 128), bf16),
        *reducer_buffers(zs, ys, xs, split),
        pltpu.VMEM((zs, fsdp, more, 128), bf16),
        *reducer_buffers(zs, ys, xs, more),
        pltpu.VMEM((rounds,) + small.shape, f32),
        pltpu.VMEM((fsdp * dp, 8, 128), f32),
        pltpu.SemaphoreType.DMA((zs,)),
        pltpu.SemaphoreType.DMA((copies,)),
        pltpu.SemaphoreType.DMA((copies,)),
        pltpu.SemaphoreType.DMA((copies,)),
        pltpu.SemaphoreType.DMA((copies,)),
        pltpu.SemaphoreType.DMA((rounds,)),
        pltpu.SemaphoreType.DMA((rounds,)),
        pltpu.SemaphoreType.DMA((fsdp * dp,)),
        pltpu.SemaphoreType.DMA((fsdp * dp,)),
    ]
    return pl.pallas_call(
        partial(backward_kernel, images, slots, heads, dp, fsdp, ff, b // images),
        grid=(b // images,),
        out_shape=[
            jax.ShapeDtypeStruct((b, slots, d), bf16),
            jax.ShapeDtypeStruct((rows, 128), f32),
            jax.ShapeDtypeStruct(small.shape, f32),
            jax.ShapeDtypeStruct((8, 128), f32),
        ],
        in_specs=[pl.BlockSpec(memory_space=pltpu.SMEM)]
        + [per(v.shape[1:]) for v in kept]
        + [whole(small.shape), whole(small.shape), whole((2, d, d)), whole((d, d)), pl.BlockSpec(memory_space=pl.ANY)],
        out_specs=[per((slots, d)), whole((rows, 128)), whole(small.shape), whole((8, 128))],
        scratch_shapes=scratch,
        compiler_params=pltpu.CompilerParams(
            dimension_semantics=("arbitrary",),
            collective_id=1,
            has_side_effects=True,
            vmem_limit_bytes=63 * 1024 * 1024,
        ),
        cost_estimate=pl.CostEstimate(flops=25_000_000_000, bytes_accessed=70_000_000, transcendentals=0),
    )(locality, *kept, small, small_part, wqk, wv, first_part)


def adamw(parameter, moment_one, moment_two, gradient, rate, decay_rate):
    first_new = beta_one * moment_one + (1.0 - beta_one) * gradient
    second_new = beta_two * moment_two + (1.0 - beta_two) * gradient * gradient
    first_hat = first_new / (1.0 - beta_one**STEP)
    second_hat = second_new / (1.0 - beta_two**STEP)
    new_value = parameter - rate * (
        first_hat / (jnp.sqrt(second_hat) + adam_eps) + decay_rate * parameter
    )
    return (new_value, first_new, second_new)


def update_kernel(heads, *refs):
    grad_ref, small_ref, norm_ref = refs[0:3]
    states = [refs[3 + 3 * k : 6 + 3 * k] for k in range(8)]
    outs = refs[27:]
    small = small_ref[...]
    norm = jnp.sqrt(jnp.sum(norm_ref[...], keepdims=True) + jnp.sum(small * small, keepdims=True)[0])
    factor = clip_limit / jnp.maximum(norm, clip_limit)
    outs[0][...] = norm
    u, w = states[1][0].shape
    fu = states[3][0].shape[0]
    o_at, split, _ = row_plan(fu, u)
    starts = {1: split, 2: o_at, 3: 0, 4: up16(fu)}

    def matrix(k, state, gradient, place):
        new_value, first_new, second_new = adamw(
            state[0][place], state[1][place], state[2][place], gradient * factor, learn_rate, weight_decay
        )
        outs[1 + 4 * k][place] = new_value
        outs[2 + 4 * k][place] = new_value.astype(bf16)
        outs[3 + 4 * k][place] = first_new
        outs[4 + 4 * k][place] = second_new

    at = split + u
    gradient = jnp.concatenate([grad_ref[at : at + u, 0:w], grad_ref[at + u : at + 2 * u, 0:w]], axis=1)
    matrix(0, states[0], gradient, ...)
    for k in (1, 2, 3, 4):
        rows = states[k][0].shape[0]
        matrix(k, states[k], grad_ref[starts[k] : starts[k] + rows, 0:w], ...)
    mine = small_ref[lax.axis_index("fsdp")]
    share = states[6][0].shape[1] // w
    row = jnp.concatenate([mine[6 + r : 7 + r, 0:w] for r in range(share)], axis=1)
    gradients = (mine[0:6, 0:w], row, small_ref[0, 6 + share : 10 + share, 0:heads])
    for k in range(3):
        state = states[5 + k]
        new_value, first_new, second_new = adamw(
            state[0][...], state[1][...], state[2][...], gradients[k] * factor, small_rate, 0.0
        )
        outs[21 + 3 * k][...] = new_value
        outs[22 + 3 * k][...] = first_new
        outs[23 + 3 * k][...] = second_new


def update(heads, grad, small, norm, states):
    shapes = [jax.ShapeDtypeStruct((1, 1), f32)]
    for k in range(5):
        shape = states[3 * k].shape
        shapes += [jax.ShapeDtypeStruct(shape, kind) for kind in (f32, bf16, f32, f32)]
    for k in range(5, 8):
        shapes += [jax.ShapeDtypeStruct(states[3 * k].shape, f32)] * 3
    return pl.pallas_call(
        partial(update_kernel, heads),
        out_shape=shapes,
        in_specs=[pl.BlockSpec(memory_space=pltpu.VMEM)] * 27,
        out_specs=[pl.BlockSpec(memory_space=pltpu.VMEM)] * len(shapes),
        compiler_params=pltpu.CompilerParams(vmem_limit_bytes=62 * 1024 * 1024),
    )(grad, small, norm, *states)


def body(
    dp,
    fsdp,
    tokens,
    keep_mask,
    cotangent,
    qk_weight,
    qk_first,
    qk_second,
    value_weight,
    value_first,
    value_second,
    out_weight,
    out_first,
    out_second,
    up_weight,
    up_first,
    up_second,
    down_weight,
    down_first,
    down_second,
    vectors,
    vectors_first,
    vectors_second,
    up_bias,
    up_bias_first,
    up_bias_second,
    locality,
    locality_first,
    locality_second,
):
    d = tokens.shape[-1]
    heads = locality.shape[1]
    ff = up_bias.shape[0] * fsdp
    images = 2 if fsdp <= 4 else 1
    vis = jnp.pad(keep_mask.astype(f32), ((0, 0), (0, PITCH - tokens.shape[1])))[:, None, :]
    everything, small, tokens, cotangent = gather_all(
        dp,
        fsdp,
        up16(4 * d // dp),
        qk_weight,
        value_weight.T,
        out_weight.T,
        vectors,
        up_bias,
        tokens,
        cotangent,
    )
    xt, qkvt, pa, pb, mixture, wqk, wv, feed = run_attend(
        dp, fsdp, tokens, vis, everything, small, up_weight.T, down_weight, locality, images
    )
    result, mixture_grad, middle_grad, first_part, small_part = run_feed(
        dp, fsdp, cotangent, vis, xt, mixture, everything, feed, small, ff, images
    )
    kept = (xt, qkvt, pa, pb, mixture_grad, middle_grad)
    token_grad, grad, small_sum, norm = run_backward(
        dp, fsdp, tokens.shape[1], kept, small, small_part, wqk, wv, first_part, locality, ff, images
    )

    def flat(v):
        return v.reshape(1, -1)

    states = [qk_weight, qk_first, qk_second]
    states += [v.T for v in (value_weight, value_first, value_second, out_weight, out_first, out_second)]
    states += [v.T for v in (up_weight, up_first, up_second)]
    states += [down_weight, down_first, down_second, vectors, vectors_first, vectors_second]
    states += [flat(up_bias), flat(up_bias_first), flat(up_bias_second), locality, locality_first, locality_second]
    outs = list(update(heads, grad, small_sum, norm, states))
    for k in range(5, 17):
        outs[k] = outs[k].T
    for k in (24, 25, 26):
        outs[k] = outs[k].reshape(up_bias.shape)
    outs[0] = outs[0].reshape(())
    return (result, token_grad, *outs)


def solution(mesh):
    placed = (
        P(("dp", "fsdp"), None, None),
        P(("dp", "fsdp"), None),
        P(("dp", "fsdp"), None, None),
        P("dp", "fsdp"),
        P("dp", "fsdp"),
        P("dp", "fsdp"),
        P("fsdp", "dp"),
        P("fsdp", "dp"),
        P("fsdp", "dp"),
        P("fsdp", "dp"),
        P("fsdp", "dp"),
        P("fsdp", "dp"),
        P("fsdp", "dp"),
        P("fsdp", "dp"),
        P("fsdp", "dp"),
        P("dp", "fsdp"),
        P("dp", "fsdp"),
        P("dp", "fsdp"),
        P(None, "fsdp"),
        P(None, "fsdp"),
        P(None, "fsdp"),
        P("fsdp"),
        P("fsdp"),
        P("fsdp"),
        P(),
        P(),
        P(),
    )
    return jax.shard_map(
        partial(body, mesh.shape["dp"], mesh.shape["fsdp"]),
        mesh=mesh,
        in_specs=placed,
        out_specs=(
            P(("dp", "fsdp"), None, None),
            P(("dp", "fsdp"), None, None),
            P(),
            P("dp", "fsdp"),
            P("dp", "fsdp"),
            P("dp", "fsdp"),
            P("dp", "fsdp"),
            P("fsdp", "dp"),
            P("fsdp", "dp"),
            P("fsdp", "dp"),
            P("fsdp", "dp"),
            P("fsdp", "dp"),
            P("fsdp", "dp"),
            P("fsdp", "dp"),
            P("fsdp", "dp"),
            P("fsdp", "dp"),
            P("fsdp", "dp"),
            P("fsdp", "dp"),
            P("fsdp", "dp"),
            P("dp", "fsdp"),
            P("dp", "fsdp"),
            P("dp", "fsdp"),
            P("dp", "fsdp"),
            P(None, "fsdp"),
            P(None, "fsdp"),
            P(None, "fsdp"),
            P("fsdp"),
            P("fsdp"),
            P("fsdp"),
            P(),
            P(),
            P(),
        ),
        check_vma=False,
    )
```

profile of v0, /device:TPU:0, one launch (start us, length us, event | category | flops | bytes accessed | tf_op | source)
XLA Modules:
  0.0 280.8 jit_solution(12865158948397253955)
XLA Ops:
  0.7 0.7 convert_element_type.5
  1.4 0.6 broadcast_in_dim.3.vis_ref
  2.0 28.0 %shard_map.506 = (bf16[8,4,224,128]{3,2,1,0:T(8,128)(2,1)}, f32[4,16,128]{2,1,0:T(8,128)}, bf16[16,196,432]{2,1,0:T(8,128)(2,1)}, bf16[16,196,432]{2,1,0:T(8,128)(2,1)}) custom-call(f32[54,216]{1,0:T(8,128)} %refs_3_.1, f32[54,108]{1,0:T(8,128)} %bitcast.32, f32[54,108]{1,0:T(8,128)} %bitcast.34, f32[6,108]{1,0:T(8,128)} %refs_18_.1, f32[1,432]{1,0:T(1,128)} %bitcast.44, ...), custom_call_target="tpu_custom_call" | custom-call | tf_op jit(solution)/shard_map/pallas_call | solution.py:323
  30.1 56.8 %shard_map.507 = (bf16[16,432,256]{2,1,0:T(8,128)(2,1)}, bf16[16,1296,256]{2,1,0:T(8,128)(2,1)}, bf16[16,9,208,256]{3,2,1,0:T(8,128)(2,1)}, bf16[16,9,208,256]{3...) custom-call(f32[4,9]{1,0:T(4,128)} %refs_24_.1, ...), custom_call_target="tpu_custom_call" | custom-call | flops 20000000000 | bytes 70000000 | tf_op jit(solution)/shard_map/pallas_call | solution.py:650
  86.9 94.1 %shard_map.508 = (bf16[16,196,432]{2,1,0:T(8,128)(2,1)}, bf16[16,432,256]{2,1,0:T(8,128)(2,1)}, bf16[16,432,256]{2,1,0:T(8,128)(2,1)}, bf16[8,4,512,128]{3,2,1,0:T(8,128)(2,1)}, f32[4,16,128]{2,1,0:T(8,128)}) custom-call(bf16[16,196,432]{2,1,0:T(8,128)(2,1)} %get-tuple-element.83.cot_ref, f32[16,1,256]{2,1,0:T(1,128)} %broadcast_in_dim.3.vis_ref, ...), custom_call_target="tpu_custom_call" | custom-call | flops 40000000000 | bytes 40000000 | tf_op jit(solution)/shard_map/pallas_call | solution.py:1002
  181.0 89.0 %shard_map.509 = (bf16[16,196,432]{2,1,0:T(8,128)(2,1)}, f32[688,128]{1,0:T(8,128)}, f32[4,16,128]{2,1,0:T(8,128)}, f32[8,128]{1,0:T(8,128)}) custom-call(f32[4,9]{1,0:T(4,128)} %refs_24_.1, bf16[16,432,256]{2,1,0:T(8,128)(2,1)} %get-tuple-element.87.xt_ref, bf16[16,1296,256]{2,1,0:T(8,128)(2,1)} %get-tuple-element.91.qkvt_ref, ...), custom_call_target="tpu_custom_call" | custom-call | flops 24999999488 | bytes 70000000 | tf_op jit(solution)/shard_map/pallas_call | solution.py:1556
  270.1 0.0 copy-start
  270.1 4.8 %copy.59 = bf16[16,196,432]{2,0,1:T(8,128)(2,1)} copy(bf16[16,196,432]{2,1,0:T(8,128)(2,1)} %get-tuple-element.134) | data formatting | bytes 5419008
  274.9 0.0 copy-done
  274.9 2.8 copy.60
  277.7 2.6 shard_map.510
  (1 shorter events, 0.0 us)
Async XLA Ops:
  270.1 4.8 %copy-start = (bf16[16,196,432]{2,1,0:T(8,128)(2,1)S(1)}, bf16[16,196,432]{2,1,0:T(8,128)(2,1)}, u32[]{:S(2)}) copy-start(bf16[16,196,432]{2,1,0:T(8,128)(2,1)} %get-tuple-element.135) | copy-start | bytes 8128516
where the time goes:
time: 282 us; the launch traced here: 281 us
  Pallas kernels  271 us (96%)
  local copies, waits for them, and re-layouts  8.25 us (3%)
    pallas_call x1, Pallas kernels, run_feed(): pl.pallas_call(partial(feed_kernel, images, slots), grid=(b // images,),...  94.1 us
    pallas_call x1, Pallas kernels, run_backward(): pl.pallas_call(partial(backward_kernel, images, slots, heads, dp, fsdp, f...  89 us
    pallas_call x1, Pallas kernels, run_attend(): pl.pallas_call(partial(attend_kernel, images, slots, heads, dp, fsdp, b /...  56.8 us
    pallas_call x1, Pallas kernels, gather_all(): pl.pallas_call(partial(gather_kernel, dp, fsdp, rows), out_shape=[jax.Sha...  28 us
    unnamed x4, local copies, waits for them, and re-layouts  7.63 us

commit v1 on v0

--- a/solution.py
+++ b/solution.py
@@ -446,8 +446,12 @@
     dn_ref,
     xt_ref,
     qkvt_ref,
-    pa_ref,
-    pb_ref,
+    pa_0,
+    pa_1,
+    pa_2,
+    pb_0,
+    pb_1,
+    pb_2,
     mixture_ref,
     wqk_ref,
     wv_ref,
@@ -584,8 +588,8 @@
             z = placed[h] + bias
             e = jnp.exp2(z - jnp.max(z, axis=0, keepdims=True))
             pb = e * (sig[h] / jnp.sum(e, axis=0, keepdims=True))
-            pa_ref[b, h] = pa.astype(bf16)
-            pb_ref[b, h] = pb.astype(bf16)
+            (pa_0, pa_1, pa_2)[h // 3][b, h % 3] = pa.astype(bf16)
+            (pb_0, pb_1, pb_2)[h // 3][b, h % 3] = pb.astype(bf16)
             mix_s[h, 0:keys, :] = (pa + pb).astype(bf16)
 
         def fc(h):
@@ -626,7 +630,7 @@
     def per(shape):
         return pl.BlockSpec((images,) + shape, lambda g: (g,) + (0,) * len(shape))
 
-    kept_shapes = [(d, PITCH), (3 * d, PITCH), (heads, keys, PITCH), (heads, keys, PITCH), (d, PITCH)]
+    kept_shapes = [(d, PITCH), (3 * d, PITCH), *[(heads // 3, keys, PITCH)] * 6, (d, PITCH)]
     scratch = [
         ((PITCH, PITCH), bf16),
         ((fsdp * 128, d), bf16),
@@ -1213,8 +1217,12 @@
     locality_ref,
     xt_ref,
     qkvt_ref,
-    pa_ref,
-    pb_ref,
+    pa_0,
+    pa_1,
+    pa_2,
+    pb_0,
+    pb_1,
+    pb_2,
     dot_ref,
     mg_ref,
     small_ref,
@@ -1376,9 +1384,9 @@
 
         def bb(h):
             g = sc_s[h % 2]
-            pa = pa_ref[b, h].astype(f32)
-            pb = pb_ref[b, h].astype(f32)
-            mix_s[h, 0:keys, :] = pa_ref[b, h] + pb_ref[b, h]
+            pa = (pa_0, pa_1, pa_2)[h // 3][b, h % 3].astype(f32)
+            pb = (pb_0, pb_1, pb_2)[h // 3][b, h % 3].astype(f32)
+            mix_s[h, 0:keys, :] = (pa_0, pa_1, pa_2)[h // 3][b, h % 3] + (pb_0, pb_1, pb_2)[h // 3][b, h % 3]
             pull_a = jnp.sum(g * pa, axis=0, keepdims=True) / cosig[h]
             pull_b = jnp.sum(g * pb, axis=0, keepdims=True) / sig[h]
             acc_gate[h : h + 1, :] += pull_b - pull_a
@@ -1694,13 +1702,13 @@
         tokens,
         cotangent,
     )
-    xt, qkvt, pa, pb, mixture, wqk, wv, feed = run_attend(
+    xt, qkvt, *soft, mixture, wqk, wv, feed = run_attend(
         dp, fsdp, tokens, vis, everything, small, up_weight.T, down_weight, locality, images
     )
     result, mixture_grad, middle_grad, first_part, small_part = run_feed(
         dp, fsdp, cotangent, vis, xt, mixture, everything, feed, small, ff, images
     )
-    kept = (xt, qkvt, pa, pb, mixture_grad, middle_grad)
+    kept = (xt, qkvt, *soft, mixture_grad, middle_grad)
     token_grad, grad, small_sum, norm = run_backward(
         dp, fsdp, tokens.shape[1], kept, small, small_part, wqk, wv, first_part, locality, ff, images
     )

time: 282 us -> 282 us (level)
  no operation moved by 1% of the time
where the time goes in v1:
time: 282 us; the launch traced here: 281 us
  Pallas kernels  271 us (96%)
  local copies, waits for them, and re-layouts  8.25 us (3%)
    pallas_call x1, Pallas kernels, run_feed(): pl.pallas_call(partial(feed_kernel, images, slots), grid=(b // images,),...  94.1 us
    pallas_call x1, Pallas kernels, run_backward(): pl.pallas_call(partial(backward_kernel, images, slots, heads, dp, fsdp, f...  89.1 us
    pallas_call x1, Pallas kernels, run_attend(): pl.pallas_call(partial(attend_kernel, images, slots, heads, dp, fsdp, b /...  56.7 us
    pallas_call x1, Pallas kernels, gather_all(): pl.pallas_call(partial(gather_kernel, dp, fsdp, rows), out_shape=[jax.Sha...  28 us
    unnamed x4, local copies, waits for them, and re-layouts  7.63 us

profile of v1, /device:TPU:0, one launch (start us, length us, event | category | flops | bytes accessed | tf_op | source)
XLA Modules:
  0.0 280.7 jit_solution(1822924769515120253)
XLA Ops:
  0.7 0.7 convert_element_type.5
  1.4 0.6 broadcast_in_dim.3.vis_ref
  2.0 28.0 %shard_map.506 = (bf16[8,4,224,128]{3,2,1,0:T(8,128)(2,1)}, f32[4,16,128]{2,1,0:T(8,128)}, bf16[16,196,432]{2,1,0:T(8,128)(2,1)}, bf16[16,196,432]{2,1,0:T(8,128)(2,1)}) custom-call(f32[54,216]{1,0:T(8,128)} %refs_3_.1, f32[54,108]{1,0:T(8,128)} %bitcast.32, f32[54,108]{1,0:T(8,128)} %bitcast.34, f32[6,108]{1,0:T(8,128)} %refs_18_.1, f32[1,432]{1,0:T(1,128)} %bitcast.44, ...), custom_call_target="tpu_custom_call" | custom-call | tf_op jit(solution)/shard_map/pallas_call | solution.py:323
  30.1 56.7 %shard_map.507 = (bf16[16,432,256]{2,1,0:T(8,128)(2,1)}, bf16[16,1296,256]{2,1,0:T(8,128)(2,1)}, bf16[16,3,208,256]{3,2,1,0:T(8,128)(2,1)}, bf16[16,3,208,256]{3...) custom-call(f32[4,9]{1,0:T(4,128)} %refs_24_.1, ...), custom_call_target="tpu_custom_call" | custom-call | flops 20000000000 | bytes 70000000 | tf_op jit(solution)/shard_map/pallas_call | solution.py:654
  86.8 94.1 %shard_map.508 = (bf16[16,196,432]{2,1,0:T(8,128)(2,1)}, bf16[16,432,256]{2,1,0:T(8,128)(2,1)}, bf16[16,432,256]{2,1,0:T(8,128)(2,1)}, bf16[8,4,512,128]{3,2,1,0:T(8,128)(2,1)}, f32[4,16,128]{2,1,0:T(8,128)}) custom-call(bf16[16,196,432]{2,1,0:T(8,128)(2,1)} %get-tuple-element.87.cot_ref, f32[16,1,256]{2,1,0:T(1,128)} %broadcast_in_dim.3.vis_ref, ...), custom_call_target="tpu_custom_call" | custom-call | flops 40000000000 | bytes 40000000 | tf_op jit(solution)/shard_map/pallas_call | solution.py:1006
  180.9 89.1 %shard_map.509 = (bf16[16,196,432]{2,1,0:T(8,128)(2,1)}, f32[688,128]{1,0:T(8,128)}, f32[4,16,128]{2,1,0:T(8,128)}, f32[8,128]{1,0:T(8,128)}) custom-call(f32[4,9]{1,0:T(4,128)} %refs_24_.1, bf16[16,432,256]{2,1,0:T(8,128)(2,1)} %get-tuple-element.91.xt_ref, bf16[16,1296,256]{2,1,0:T(8,128)(2,1)} %get-tuple-element.95.qkvt_ref, ...), custom_call_target="tpu_custom_call" | custom-call | flops 24999999488 | bytes 70000000 | tf_op jit(solution)/shard_map/pallas_call | solution.py:1564
  270.0 0.0 copy-start
  270.0 4.8 %copy.59 = bf16[16,196,432]{2,0,1:T(8,128)(2,1)} copy(bf16[16,196,432]{2,1,0:T(8,128)(2,1)} %get-tuple-element.142) | data formatting | bytes 5419008
  274.8 0.0 copy-done
  274.8 2.8 copy.60
  277.6 2.6 shard_map.510
  (1 shorter events, 0.0 us)
Async XLA Ops:
  270.0 4.8 %copy-start = (bf16[16,196,432]{2,1,0:T(8,128)(2,1)S(1)}, bf16[16,196,432]{2,1,0:T(8,128)(2,1)}, u32[]{:S(2)}) copy-start(bf16[16,196,432]{2,1,0:T(8,128)(2,1)} %get-tuple-element.143) | copy-start | bytes 8128516
